TPU v7x, 32 devices: a whole 2x2x4 slice. The times are simulated.
32 devices in a mesh: groups: 2 (over y), ep: 8 (over z, x), dp: 2 (over core).
Axes of the slice: x: 2, y: 2, z: 4, core: 2. Of those that a mesh axis runs over, the one named last changes fastest.
Arguments:
- out_grad: bfloat16 [4096, 2048], P(('groups', 'ep', 'dp')), parts along dimension 0, may hold values from -6 to 6
- gate_prob: float32 [4096, 8], P(('groups', 'ep', 'dp')), parts along dimension 0, may hold values from 0.05 to 0.5
- saved_hidden: bfloat16 [4096, 8, 768], P(('groups', 'ep', 'dp')), parts along dimension 0, may hold values from -6 to 6
- slot_weight: bfloat16 [16, 768, 2048], P(('ep', 'dp')), may hold values from -0.125 to 0.125
- pair_slot: int32 [4096, 8], P(('groups', 'ep', 'dp')), parts along dimension 0, may hold values from 0 to 15, all different within a row; in each aligned block of 128 rows (0 to 127, 128 to 255, ...) at most 80 rows name the same one
- slot_expert: int32 [32], P('groups'), parts along dimension 0, may hold values from 0 to 7, as said below
Outputs:
- hidden_grad: bfloat16 [4096, 8, 768], P(('groups', 'ep', 'dp')), parts along dimension 0
- left_gram: bfloat16 [16, 768, 768], P(('groups', 'ep'), 'dp'), parts along dimension 0
- right_gram: bfloat16 [16, 2048, 2048], P(('groups', 'ep'), 'dp'), parts along dimension 0
There are 2 independent parts, one for each index of `groups`. A program takes and returns all parts, laid end to end along the dimension named above; an argument that names none is the same for every part. Nothing has to cross between parts.
Inputs may be any that keep to these rules, and one draw needn't show every extreme that they name: `pair_slot`: each token names 8 different slots; the tokens of one device name one slot at most 80 times. Two slots of a token may host the same expert. `slot_expert`: slot 2 e hosts expert e. Slot 2 e + 1 hosts expert e, or expert e - 1 when e is odd.
All inputs are finite; a program needn't handle non-finite values.
Results may differ from a plain program's by a relative error of at most 0.0065.
Values may be sent and summed in bfloat16 or wider, within the bound.
A program may use at most 128 MiB of HBM per device.

v0:
```python
import jax
import jax.numpy as jnp
from jax import lax
from jax.sharding import PartitionSpec as P

D = 2048
FF = 768


def shifted(array, axis, by):
    peers = lax.axis_size(axis)
    pairs = [(i, i + by) for i in range(peers) if 0 <= i + by < peers]
    return lax.ppermute(array, axis, pairs)


def route_table(pair_slot, slot_count, capacity):
    npairs = pair_slot.shape[0] * pair_slot.shape[1]
    target = pair_slot.reshape(npairs)
    onehot = (target[:, None] == jnp.arange(slot_count, dtype=jnp.int32)[None, :]).astype(jnp.int32)
    earlier = jnp.cumsum(onehot, axis=0) - onehot
    position = jnp.sum(earlier * onehot, axis=1)
    bucket = target * capacity + position
    selector = (
        bucket[None, :] == jnp.arange(slot_count * capacity, dtype=jnp.int32)[:, None]
    ).astype(jnp.int32)
    filled = jnp.sum(selector, axis=1) > 0
    source = jnp.sum(selector * jnp.arange(npairs, dtype=jnp.int32)[None, :], axis=1)
    return (bucket, filled, source)


def local(out_grad, gate_prob, saved_hidden, slot_weight, pair_slot, slot_expert):
    tokens, choose = pair_slot.shape
    width = out_grad.shape[1]
    hidden_width = saved_hidden.shape[2]
    slot_count = slot_expert.shape[0]
    ep_count = lax.axis_size("ep")
    dp_count = lax.axis_size("dp")
    capacity = max(2, 5 * tokens * choose // (4 * slot_count))
    bucket, filled, source = route_table(pair_slot, slot_count, capacity)
    gate_flat = gate_prob.reshape(tokens * choose)
    hidden_flat = saved_hidden.reshape(tokens * choose, hidden_width)
    scaled = out_grad[source // choose].astype(jnp.float32) * gate_flat[source][:, None]
    grad_rows = jnp.where(filled[:, None], scaled, jnp.zeros((), jnp.float32)).astype(jnp.bfloat16)
    held_rows = jnp.where(filled[:, None], hidden_flat[source], jnp.zeros((), jnp.bfloat16))
    grad_recv, held_recv = (
        lax.all_to_all(
            grad_rows.reshape(slot_count, capacity, width),
            ("ep", "dp"),
            split_axis=0,
            concat_axis=0,
            tiled=True,
        ),
        lax.all_to_all(
            held_rows.reshape(slot_count, capacity, hidden_width),
            ("ep", "dp"),
            split_axis=0,
            concat_axis=0,
            tiled=True,
        ),
    )
    flat_grad = grad_recv.reshape(slot_count * capacity, width)
    flat_held = held_recv.reshape(slot_count * capacity, hidden_width)
    input_grads = lax.dot_general(
        flat_grad, slot_weight[0], (((1,), (1,)), ((), ())), preferred_element_type=jnp.float32
    ).astype(jnp.bfloat16)
    returned = lax.all_to_all(
        input_grads.reshape(slot_count, capacity, hidden_width),
        ("ep", "dp"),
        split_axis=0,
        concat_axis=0,
        tiled=True,
    )
    hidden_grad = returned.reshape(slot_count * capacity, hidden_width)[bucket].reshape(
        tokens, choose, hidden_width
    )
    partial_value = lax.dot_general(
        flat_held, flat_grad, (((0,), (0,)), ((), ())), preferred_element_type=jnp.float32
    ).astype(jnp.bfloat16)
    ep_index = lax.axis_index("ep")
    dp_index = lax.axis_index("dp")
    my_slot = ep_index * dp_count + dp_index
    hosted = slot_expert[my_slot]
    own_term = jnp.where(
        hosted == ep_index, partial_value.astype(jnp.float32), jnp.zeros((), jnp.float32)
    )
    spare = jnp.where(hosted == ep_index, jnp.zeros((), jnp.bfloat16), partial_value)
    arrived = shifted(spare, "ep", -1)
    sender = jnp.minimum(my_slot + dp_count, slot_count - 1)
    usable = (slot_expert[sender] == ep_index) & (ep_index + 1 < ep_count)
    neighbour = jnp.where(usable, arrived.astype(jnp.float32), jnp.zeros((), jnp.float32))
    expert_grad = lax.psum(own_term + neighbour, "dp")
    rounded = expert_grad.astype(jnp.bfloat16)
    ff_rows = hidden_width // dp_count
    left_rows = lax.dynamic_slice_in_dim(rounded, dp_index * ff_rows, ff_rows, 0)
    left = (
        lax.dot_general(
            left_rows, rounded, (((1,), (1,)), ((), ())), preferred_element_type=jnp.float32
        )
        / D
    )
    width_rows = width // dp_count
    right_cols = lax.dynamic_slice_in_dim(rounded, dp_index * width_rows, width_rows, 1)
    right = (
        lax.dot_general(
            right_cols, rounded, (((0,), (0,)), ((), ())), preferred_element_type=jnp.float32
        )
        / FF
    )
    return (hidden_grad, left.astype(jnp.bfloat16)[None], right.astype(jnp.bfloat16)[None])


def solution(mesh):
    return jax.shard_map(
        local,
        mesh=mesh,
        in_specs=(
            P(("groups", "ep", "dp"), None),
            P(("groups", "ep", "dp"), None),
            P(("groups", "ep", "dp"), None, None),
            P(("ep", "dp"), None, None),
            P(("groups", "ep", "dp"), None),
            P("groups"),
        ),
        out_specs=(
            P(("groups", "ep", "dp"), None, None),
            P(("groups", "ep"), "dp", None),
            P(("groups", "ep"), "dp", None),
        ),
        check_vma=False,
    )
```

profile of v0, /device:TPU:21, one launch (start us, length us, event | category | flops | bytes accessed | tf_op | source)
XLA Modules:
  0.0 334.2 jit_solution(11237510224685191612)
XLA Ops:
  0.6 0.0 copy-start
  0.6 0.9 copy.17
  1.6 0.1 reshape.177
  1.7 0.1 eq.46
  1.8 4.5 %reduce-window.6 = s32[16,8,128]{2,1,0:T(8,128)S(1)} reduce-window(s32[16,8,128]{2,1,0:T(8,128)S(1)} %fusion.19, s32[]{:T(128)} %constant.23.clone.1), window={size=1x1x128 pad=0_0x0_0x127_0}, to_apply=%region_0.0 | reduce-window | flops 2080768 | bytes 131076 | tf_op jit(solution)/shard_map/reduce-window
  6.3 0.1 slice.16
  6.4 0.1 copy.19
  6.5 0.1 copy.20
  6.6 0.1 broadcast_add_fusion
  6.8 1.6 convert_reduce_fusion
  8.4 0.1 gt.11
  8.5 0.1 fusion.20
  8.6 7.4 %gather_fusion.3 = bf16[1280,768]{1,0:T(8,128)(2,1)} fusion(bf16[1024,768]{1,0:T(8,128)(2,1)} %bitcast.44, s32[2048]{0:T(1024)S(1)} %get-tuple-element.11), kind=kCustom, calls=%fused_computation.3 | custom fusion | bytes 3937280 | tf_op jit(solution)/shard_map/gather | solution.py:44
  16.0 0.0 copy-start.3
  16.0 3.1 broadcast_select_fusion.1
  19.0 6.5 %all-to-all-start.2 = ((bf16[16,80,768]{2,1,0:T(8,128)(2,1)}), bf16[16,80,768]{2,1,0:T(8,128)(2,1)}, u32[]{:S(2)}, u32[]{:S(2)}) async-start(bf16[16,80,768]{2,1,0:T(8,128)(2,1)} %broadcast_select_fusion.1), calls=%async_computation.2 | async-start | bytes 3932160 | tf_op jit(solution)/shard_map/all_to_all | solution.py:53
  25.5 0.0 copy-done.3
  25.5 0.1 copy.21
  25.6 0.1 reshape.179
  25.7 5.0 %gather_fusion.1 = f32[1280]{0:T(1024)S(1)} fusion(f32[1024]{0:T(1024)S(1)} %reshape.179, s32[2048]{0:T(1024)S(1)} %get-tuple-element.11), kind=kCustom, calls=%fused_computation.1 | custom fusion | bytes 15360 | tf_op jit(solution)/shard_map/gather | solution.py:42
  30.7 0.1 mul.60
  30.7 11.9 %gather_fusion = bf16[1280,2048]{1,0:T(8,128)(2,1)} fusion(bf16[128,2048]{1,0:T(8,128)(2,1)} %param.6, s32[2048]{0:T(1024)S(1)} %get-tuple-element.12), kind=kCustom, calls=%fused_computation | custom fusion | bytes 10490880 | tf_op jit(solution)/shard_map/gather | solution.py:42
  42.7 6.1 %fusion.1 = bf16[16,80,2048]{2,1,0:T(8,128)(2,1)} fusion(bf16[16,80,2048]{2,1,0:T(8,128)(2,1)} %bitcast.45, f32[16,80]{1,0:T(8,128)S(1)} %mul.60, pred[16,80]{1,0:T(8,128)(4,1)S(1)} %gt.11), kind=kLoop, calls=%fused_computation.6 | loop fusion | flops 10485760 | bytes 10492160 | tf_op jit(solution)/shard_map/convert_element_type | solution.py:43
  48.8 0.0 copy-start.4
  48.8 21.1 %all-to-all-done.2 = bf16[16,80,768]{2,1,0:T(8,128)(2,1)} async-done(((bf16[16,80,768]{2,1,0:T(8,128)(2,1)}), bf16[16,80,768]{2,1,0:T(8,128)(2,1)}, u32[]{:S(2)}, u32[]{:S(2)}) %all-to-all-start.2) | async-done | bytes 1966112 | tf_op jit(solution)/shard_map/all_to_all | solution.py:53
  69.9 5.2 %all-to-all-start = ((bf16[16,80,2048]{2,1,0:T(8,128)(2,1)}), bf16[16,80,2048]{2,1,0:T(8,128)(2,1)}, u32[]{:S(2)}, u32[]{:S(2)}) async-start(bf16[16,80,2048]{2,1,0:T(8,128)(2,1)} %fusion.1), calls=%async_computation | async-start | bytes 10485760 | tf_op jit(solution)/shard_map/all_to_all | solution.py:46
  75.1 0.0 copy-done.4
  75.1 0.6 fusion.24
  76.4 0.0 copy-start.2
  76.4 113.4 %all-to-all-done = bf16[16,80,2048]{2,1,0:T(8,128)(2,1)} async-done(((bf16[16,80,2048]{2,1,0:T(8,128)(2,1)}), bf16[16,80,2048]{2,1,0:T(8,128)(2,1)}, u32[]{:S(2)}, u32[]{:S(2)}) %all-to-all-start) | async-done | bytes 5242912 | tf_op jit(solution)/shard_map/all_to_all | solution.py:46
  189.8 10.1 %broadcast_select_fusion = (bf16[768,2048]{1,0:T(8,128)(2,1)}, bf16[768,2048]{1,0:T(8,128)(2,1)}) fusion(pred[]{:T(512)S(6)} %eq.53, bf16[16,80,768]{2,1,0:T(8,128)(2,1)} %all-to-all-done.2, bf16[16,80,2048]{2,1,0:T(8,128)(2,1)} %all-to-all-done), kind=kOutput, calls=%fused_computation.16 | convolution fusion | flops 4029677568 | bytes 13500417 | tf_op jit(solution)/shard_map/dot_general | solution.py:76
  199.9 3.5 %collective-permute-start = (bf16[768,2048]{1,0:T(8,128)(2,1)}, bf16[768,2048]{1,0:T(8,128)(2,1)}, u32[]{:S(2)}, u32[]{:S(2)}) collective-permute-start(bf16[768,2048]{1,0:T(8,128)(2,1)} %get-tuple-element.9), channel_id=1, source_target_pairs={{2,0},{4,2},{6,4},{8,6},{10,8},{12,10},{14,12},{3,1},{5,3},{7,5},{... | collective-permute-start | bytes 9437192 | tf_op jit(solution)/shard_map/ppermute | solution.py:13
  204.0 0.0 copy-done.2
  204.1 0.1 copy.22
  204.2 0.1 mul.65
  204.3 0.0 copy-done
  204.3 8.1 %convolution_convert_fusion = bf16[1280,768]{1,0:T(8,128)(2,1)} fusion(bf16[1280,2048]{1,0:T(8,128)(2,1)} %bitcast.3, bf16[1,768,2048]{2,1,0:T(8,128)(2,1)S(1)} %copy-done), kind=kOutput, calls=%fused_computation.13 | convolution fusion | flops 4027514880 | bytes 10354688 | tf_op jit(solution)/shard_map/dot_general | solution.py:63
  212.4 4.7 %all-to-all-start.1 = ((bf16[16,80,768]{2,1,0:T(8,128)(2,1)}), bf16[16,80,768]{2,1,0:T(8,128)(2,1)}, u32[]{:S(2)}, u32[]{:S(2)}) async-start(bf16[16,80,768]{2,1,0:T(8,128)(2,1)} %bitcast.47), calls=%async_computation.1 | async-start | bytes 3932160 | tf_op jit(solution)/shard_map/all_to_all | solution.py:66
  217.2 69.6 %collective-permute-done = bf16[768,2048]{1,0:T(8,128)(2,1)} collective-permute-done((bf16[768,2048]{1,0:T(8,128)(2,1)}, bf16[768,2048]{1,0:T(8,128)(2,1)}, u32[]{:S(2)}, u32[]{:S(2)}) %collective-permute-start) | collective-permute-done | bytes 3145760 | tf_op jit(solution)/shard_map/ppermute | solution.py:13
  286.8 6.9 %select_add_fusion = f32[768,2048]{1,0:T(8,128)} fusion(bf16[768,2048]{1,0:T(8,128)(2,1)} %collective-permute-done, bf16[768,2048]{1,0:T(8,128)(2,1)} %get-tuple-element.10, pred[]{:T(512)S(6)} %and.25, pred[]{:T(512)S(6)} %eq.53), kind=kLoop, calls=%fused_computation.9 | loop fusion | flops 7864320 | bytes 12582914 | tf_op jit(solution)/shard_map/add | solution.py:91
  293.7 23.3 %all-reduce.1 = bf16[768,2048]{1,0:T(8,128)(2,1)} all-reduce(f32[768,2048]{1,0:T(8,128)} %select_add_fusion), channel_id=1, replica_groups=mesh['groups'=2,'ep'=8,'dp'=2] {'dp'}, use_global_device_ids=true, to_apply=%region_5.6 | all-reduce | flops 1572864 | bytes 9437184 | tf_op jit(solution)/shard_map/psum | solution.py:91
  317.0 0.0 copy-start.1
  317.0 4.8 %fusion.13 = bf16[1,384,768]{2,1,0:T(8,128)(2,1)} fusion(bf16[768,2048]{1,0:T(8,128)(2,1)} %all-reduce.1, s32[]{:T(128)S(6)} %select_n.98), kind=kOutput, calls=%fused_computation.23 | convolution fusion | flops 1208549376 | bytes 5308420 | tf_op jit(solution)/shard_map/dot_general | solution.py:96
  321.7 0.0 copy-done.1
  321.7 5.1 %fusion.2 = bf16[1,1024,2048]{2,1,0:T(8,128)(2,1)} fusion(bf16[768,2048]{1,0:T(8,128)(2,1)S(1)} %copy-done.1, s32[]{:T(128)S(6)} %select_n.99), kind=kOutput, calls=%fused_computation.14 | convolution fusion | flops 3225419776 | bytes 8912900 | tf_op jit(solution)/shard_map/dot_general | solution.py:104
  326.9 0.0 all-to-all-done.1
  326.9 7.4 %gather_fusion.2 = bf16[1024,768]{1,0:T(8,128)(2,1)} fusion(bf16[1280,768]{1,0:T(8,128)(2,1)} %bitcast.6, s32[1024]{0:T(1024)S(1)} %broadcast_clamp_fusion), kind=kCustom, calls=%fused_computation.2 | custom fusion | bytes 3149824 | tf_op jit(solution)/shard_map/gather | solution.py:73
  (10 shorter events, 0.1 us)
Async XLA Ops:
  0.6 203.7 %copy-start = (bf16[1,768,2048]{2,1,0:T(8,128)(2,1)S(1)}, bf16[1,768,2048]{2,1,0:T(8,128)(2,1)}, u32[]{:S(2)}) copy-start(bf16[1,768,2048]{2,1,0:T(8,128)(2,1)} %param.9) | copy-start | bytes 9437188
  16.0 9.5 %copy-start.3 = (f32[128,8]{0,1:T(8,128)S(1)}, f32[128,8]{0,1:T(8,128)}, u32[]{:S(2)}) copy-start(f32[128,8]{0,1:T(8,128)} %param.7) | copy-start | bytes 12292
  19.0 50.9 %all-to-all-start.2 = ((bf16[16,80,768]{2,1,0:T(8,128)(2,1)}), bf16[16,80,768]{2,1,0:T(8,128)(2,1)}, u32[]{:S(2)}, u32[]{:S(2)}) async-start(bf16[16,80,768]{2,1,0:T(8,128)(2,1)} %broadcast_select_fusion.1), calls=%async_computation.2 | async-start | bytes 3932160 | tf_op jit(solution)/shard_map/all_to_all | solution.py:53
  48.8 26.3 %copy-start.4 = (s32[16]{0:T(128)S(1)}, s32[16]{0:T(128)}, u32[]{:S(2)}) copy-start(s32[16]{0:T(128)} %param.11) | copy-start | bytes 196
  69.9 119.8 %all-to-all-start = ((bf16[16,80,2048]{2,1,0:T(8,128)(2,1)}), bf16[16,80,2048]{2,1,0:T(8,128)(2,1)}, u32[]{:S(2)}, u32[]{:S(2)}) async-start(bf16[16,80,2048]{2,1,0:T(8,128)(2,1)} %fusion.1), calls=%async_computation | async-start | bytes 10485760 | tf_op jit(solution)/shard_map/all_to_all | solution.py:46
  76.4 127.7 %copy-start.2 = (s32[128,8]{0,1:T(8,128)S(1)}, s32[128,8]{0,1:T(8,128)}, u32[]{:S(2)}) copy-start(s32[128,8]{0,1:T(8,128)} %param.10) | copy-start | bytes 12292
  199.9 86.9 %collective-permute-start = (bf16[768,2048]{1,0:T(8,128)(2,1)}, bf16[768,2048]{1,0:T(8,128)(2,1)}, u32[]{:S(2)}, u32[]{:S(2)}) collective-permute-start(bf16[768,2048]{1,0:T(8,128)(2,1)} %get-tuple-element.9), channel_id=1, source_target_pairs={{2,0},{4,2},{6,4},{8,6},{10,8},{12,10},{14,12},{3,1},{5,3},{7,5},{... | collective-permute-start | bytes 9437192 | tf_op jit(solution)/shard_map/ppermute | solution.py:13
  212.4 114.5 %all-to-all-start.1 = ((bf16[16,80,768]{2,1,0:T(8,128)(2,1)}), bf16[16,80,768]{2,1,0:T(8,128)(2,1)}, u32[]{:S(2)}, u32[]{:S(2)}) async-start(bf16[16,80,768]{2,1,0:T(8,128)(2,1)} %bitcast.47), calls=%async_computation.1 | async-start | bytes 3932160 | tf_op jit(solution)/shard_map/all_to_all | solution.py:66
  317.0 4.8 %copy-start.1 = (bf16[768,2048]{1,0:T(8,128)(2,1)S(1)}, bf16[768,2048]{1,0:T(8,128)(2,1)}, u32[]{:S(2)}) copy-start(bf16[768,2048]{1,0:T(8,128)(2,1)} %all-reduce.1) | copy-start | bytes 9437188
where the time goes:
time: 335 us; the launch traced here: 334 us
  waiting for transfers between devices  204 us (61%)
  local copies, waits for them, and re-layouts  34.2 us (10%)
  matrix products  28 us (8%)
  blocking collectives  23.3 us (7%)
  other arithmetic  22.5 us (7%)
  starting transfers between devices  19.9 us (6%)
    all_to_all x1, waiting for transfers between devices, local(): lax.all_to_all(grad_rows.reshape(slot_count, capacity, width), ('ep', 'dp...  113 us
    ppermute x1, waiting for transfers between devices, shifted(): return lax.ppermute(array, axis, pairs)  69.6 us
    psum x1, blocking collectives, local(): expert_grad = lax.psum(own_term + neighbour, 'dp')  23.3 us
    all_to_all x1, waiting for transfers between devices, local(): lax.all_to_all(held_rows.reshape(slot_count, capacity, hidden_width), ('e...  21.1 us
    gather x1, local copies, waits for them, and re-layouts, local(): out_grad[source // choose].astype(jnp.float32) * gate_flat[source][:, None]  11.9 us
    dot_general x1, matrix products, local(): lax.dot_general(flat_held, flat_grad, (((0,), (0,)), ((), ())), preferred...  10.1 us
    dot_general x1, matrix products, local(): lax.dot_general(flat_grad, slot_weight[0], (((1,), (1,)), ((), ())), pref...  8.09 us
    gather x1, local copies, waits for them, and re-layouts, local(): hidden_flat[source]  7.4 us
  transfers between devices with their start and end apart: 4, of which 3 were waited for; matrix products, arithmetic and copies ran while one was open for 15% of the time, Pallas kernels for 0%

commit v1 on v0

v1 whole, which is shorter than its diff:
```python
import jax
import jax.numpy as jnp
from jax import lax
from jax.sharding import PartitionSpec as P

AXES = ("ep", "dp")
BLOCK = 16


def combined(gate_prob, expert_of_pair, saved_hidden, experts):
    tokens, choose = gate_prob.shape
    width = saved_hidden.shape[2]
    blocks = tokens // BLOCK
    pairs = BLOCK * choose
    gates = gate_prob.reshape(blocks, 1, 1, pairs)
    hosts = expert_of_pair.reshape(blocks, 1, 1, pairs)
    owner = jnp.arange(pairs, dtype=jnp.int32) // choose
    keep = (hosts == jnp.arange(experts, dtype=jnp.int32)[None, :, None, None]) & (
        owner[None, None, None, :] == jnp.arange(BLOCK, dtype=jnp.int32)[None, None, :, None]
    )
    high = lax.reduce_precision(gates, 8, 7)
    low = gates - high
    zero = jnp.zeros((), jnp.float32)
    weights = jnp.concatenate(
        [jnp.where(keep, high, zero), jnp.where(keep, low, zero)], axis=3
    ).astype(jnp.bfloat16)
    hidden = saved_hidden.reshape(blocks, pairs, width)
    hidden = jnp.concatenate([hidden, hidden], axis=1)
    out = lax.dot_general(
        weights.reshape(blocks, experts * BLOCK, 2 * pairs),
        hidden,
        (((2,), (1,)), ((0,), (0,))),
        preferred_element_type=jnp.float32,
    ).astype(jnp.bfloat16)
    return out.reshape(blocks, experts, BLOCK, width).transpose(1, 0, 2, 3).reshape(
        experts, tokens, width
    )


def local(out_grad, gate_prob, saved_hidden, slot_weight, pair_slot, slot_expert):
    tokens, choose = pair_slot.shape
    width = out_grad.shape[1]
    hidden_width = saved_hidden.shape[2]
    slot_count = slot_expert.shape[0]
    ep_count = lax.axis_size("ep")
    dp_count = lax.axis_size("dp")
    half = hidden_width // dp_count
    capacity = max(2, 5 * tokens * choose // (4 * slot_count))
    dp_index = lax.axis_index("dp")

    everyone = lax.all_gather(out_grad, AXES, axis=0, tiled=True)

    slots = jnp.arange(slot_count, dtype=jnp.int32)
    named = pair_slot[:, :, None] == slots[None, None, :]
    dense_gate = jnp.sum(jnp.where(named, gate_prob[:, :, None], 0.0), axis=1).T
    gates = lax.all_to_all(dense_gate, AXES, split_axis=0, concat_axis=0, tiled=True)

    expert_of_pair = jnp.sum(jnp.where(named, slot_expert[None, None, :], 0), axis=2)
    sums = combined(gate_prob, expert_of_pair, saved_hidden, ep_count)
    sums = (
        sums.reshape(ep_count, tokens, dp_count, half)
        .transpose(0, 2, 1, 3)
        .reshape(slot_count, tokens, half)
    )
    sums = lax.all_to_all(sums, AXES, split_axis=0, concat_axis=0, tiled=True)

    used = gates > 0
    before = (
        jnp.arange(tokens)[:, None] < jnp.arange(tokens)[None, :]
    ).astype(jnp.bfloat16)
    place = lax.dot_general(
        used.astype(jnp.bfloat16), before, (((1,), (0,)), ((), ())),
        preferred_element_type=jnp.float32,
    ).astype(jnp.int32)
    place = jnp.where(used, place, -1)
    select = place[:, None, :] == jnp.arange(capacity, dtype=jnp.int32)[None, :, None]
    rows = lax.dot_general(
        select.astype(jnp.bfloat16),
        everyone.reshape(slot_count, tokens, width),
        (((2,), (1,)), ((0,), (0,))),
        preferred_element_type=jnp.float32,
    )
    row_gate = jnp.sum(jnp.where(select, gates[:, None, :], 0.0), axis=2)
    pair_grad = (rows * row_gate[:, :, None]).astype(jnp.bfloat16)
    input_grads = lax.dot_general(
        pair_grad.reshape(slot_count * capacity, width),
        slot_weight[0],
        (((1,), (1,)), ((), ())),
        preferred_element_type=jnp.float32,
    ).astype(jnp.bfloat16)
    returned = lax.all_to_all(
        input_grads.reshape(slot_count, capacity, hidden_width),
        AXES, split_axis=0, concat_axis=0, tiled=True,
    )

    grad_half = lax.dot_general(
        sums.reshape(slot_count * tokens, half),
        everyone,
        (((0,), (0,)), ((), ())),
        preferred_element_type=jnp.float32,
    ).astype(jnp.bfloat16)
    rounded = lax.all_gather(grad_half, "dp", axis=0, tiled=True)
    left = (
        lax.dot_general(
            grad_half, rounded, (((1,), (1,)), ((), ())), preferred_element_type=jnp.float32
        )
        / width
    )
    width_rows = width // dp_count
    right_cols = lax.dynamic_slice_in_dim(rounded, dp_index * width_rows, width_rows, 1)
    right = (
        lax.dot_general(
            right_cols, rounded, (((0,), (0,)), ((), ())), preferred_element_type=jnp.float32
        )
        / hidden_width
    )

    served = jnp.any(named, axis=1).astype(jnp.bfloat16)
    earlier = lax.dot_general(
        before, served, (((0,), (0,)), ((), ())), preferred_element_type=jnp.float32
    ).astype(jnp.int32)
    position = jnp.sum(
        jnp.where(named, (earlier + slots * capacity)[:, None, :], 0), axis=2
    ).reshape(tokens * choose)
    pick = (
        position[:, None] == jnp.arange(slot_count * capacity, dtype=jnp.int32)[None, :]
    ).astype(jnp.bfloat16)
    hidden_grad = lax.dot_general(
        pick,
        returned.reshape(slot_count * capacity, hidden_width),
        (((1,), (0,)), ((), ())),
        preferred_element_type=jnp.float32,
    ).astype(jnp.bfloat16).reshape(tokens, choose, hidden_width)
    return (hidden_grad, left.astype(jnp.bfloat16)[None], right.astype(jnp.bfloat16)[None])


def solution(mesh):
    return jax.shard_map(
        local,
        mesh=mesh,
        in_specs=(
            P(("groups", "ep", "dp"), None),
            P(("groups", "ep", "dp"), None),
            P(("groups", "ep", "dp"), None, None),
            P(("ep", "dp"), None, None),
            P(("groups", "ep", "dp"), None),
            P("groups"),
        ),
        out_specs=(
            P(("groups", "ep", "dp"), None, None),
            P(("groups", "ep"), "dp", None),
            P(("groups", "ep"), "dp", None),
        ),
        check_vma=False,
    )
```

time: 335 us -> 191 us (0.57)
  waiting for transfers between devices: 204 us -> 104 us
  local copies, waits for them, and re-layouts: 34.2 us -> 9.76 us
  blocking collectives: 23.3 us -> 0 us
  other arithmetic: 22.5 us -> 3.59 us
  between operations: 2.09 us -> 14.2 us
  matrix products: 28 us -> 36.9 us
    ppermute x1 -> x0, waiting for transfers between devices: 69.6 us -> none  [shifted(): return lax.ppermute(array, axis, pairs)]
    all_to_all x3, waiting for transfers between devices: 135 us -> 102 us  [the longest x1 67.7 us: local(): sums = lax.all_to_all(sums, AXES, split_axis=0, concat_axis=0, tiled=True)]
    gather x4 -> x0, local copies, waits for them, and re-layouts: 31.7 us -> none  [the longest x1 11.9 us: local(): out_grad[source // choose].astype(jnp.float32) * gate_flat[source][:, None]]
    psum x1 -> x0, blocking collectives: 23.3 us -> none  [local(): expert_grad = lax.psum(own_term + neighbour, 'dp')]
    dot_general x3 -> x8, matrix products: 22.9 us -> 31.8 us  [the longest x1 8.49 us: local(): lax.dot_general(sums.reshape(slot_count * tokens, half), everyone, (((0,)...]
    add x2 -> x0, other arithmetic: 6.93 us -> none  [the longest x1 6.93 us: local(): expert_grad = lax.psum(own_term + neighbour, 'dp')]
    convert_element_type x2 -> x0, other arithmetic: 6.14 us -> none  [the longest x1 6.13 us: local(): jnp.where(filled[:, None], scaled, jnp.zeros((), jnp.float32))]
    all_to_all x3, starting transfers between devices: 16.4 us -> 21.8 us  [the longest x1 9.32 us: local(): lax.all_to_all(input_grads.reshape(slot_count, capacity, hidden_width), A...]
  transfers between devices with their start and end apart: 4 -> 5, of which waited for: 3 -> 3; matrix products, arithmetic and copies ran while one was open for 15% -> 19% of each run, Pallas kernels for 0% -> 0%
where the time goes in v1:
time: 191 us; the launch traced here: 190 us
  waiting for transfers between devices  104 us (54%)
  matrix products  36.9 us (19%)
  starting transfers between devices  21.9 us (11%)
  between operations  14.2 us (7%)
  local copies, waits for them, and re-layouts  9.76 us (5%)
  other arithmetic  3.59 us (2%)
    all_to_all x1, waiting for transfers between devices, local(): sums = lax.all_to_all(sums, AXES, split_axis=0, concat_axis=0, tiled=True)  67.7 us
    all_to_all x1, waiting for transfers between devices, local(): lax.all_to_all(input_grads.reshape(slot_count, capacity, hidden_width), A...  34.3 us
    all_to_all x1, starting transfers between devices, local(): lax.all_to_all(input_grads.reshape(slot_count, capacity, hidden_width), A...  9.32 us
    dot_general x1, matrix products, local(): lax.dot_general(sums.reshape(slot_count * tokens, half), everyone, (((0,)...  8.49 us
    all_to_all x1, starting transfers between devices, local(): lax.all_to_all(dense_gate, AXES, split_axis=0, concat_axis=0, tiled=True)  6.47 us
    all_to_all x1, starting transfers between devices, local(): sums = lax.all_to_all(sums, AXES, split_axis=0, concat_axis=0, tiled=True)  6.02 us
    dot_general x1, matrix products, local(): lax.dot_general(pair_grad.reshape(slot_count * capacity, width), slot_wei...  5.58 us
    dot_general x1, matrix products, local(): lax.dot_general(right_cols, rounded, (((0,), (0,)), ((), ())), preferred_...  5.12 us
  transfers between devices with their start and end apart: 5, of which 3 were waited for; matrix products, arithmetic and copies ran while one was open for 19% of the time, Pallas kernels for 0%

profile of v1, /device:TPU:21, one launch (start us, length us, event | category | flops | bytes accessed | tf_op | source)
XLA Modules:
  0.0 190.1 jit_solution(7684175014091120000)
XLA Ops:
  7.2 0.0 copy-start
  7.2 0.0 all-gather.3.cloned.1.call-start
  7.2 0.7 all-gather.3.cloned.1.call-update
  7.9 1.5 select_reduce_fusion.2
  9.4 6.5 %all-to-all-start = ((f32[16,1,128]{2,1,0:T(1,128)}), f32[16,1,128]{2,1,0:T(1,128)S(1)}, u32[]{:S(2)}, u32[]{:S(2)}) async-start(f32[16,1,128]{2,1,0:T(1,128)} %bitcast.2), calls=%async_computation | async-start | bytes 16384 | tf_op jit(solution)/shard_map/all_to_all | solution.py:56
  15.9 0.8 copy.27
  16.7 0.1 reshape.126
  16.8 0.7 fusion.22
  17.5 0.1 fusion.17
  17.6 0.8 select_reduce_fusion.1
  18.4 0.1 copy.26
  18.5 0.1 eq.89
  18.7 0.1 select_convert_fusion.1
  18.8 2.7 %fusion.8 = bf16[8,128,768]{2,1,0:T(8,128)(2,1)S(1)} fusion(bf16[8,128,768]{2,1,0:T(8,128)(2,1)} %bitcast.55, bf16[8,128,128]{2,1,0:T(8,128)(2,1)S(1)} %get-tuple-element.6, bf16[8,128,128]{2,1,0:T(8,128)(2,1)S(1)} %get-tuple-element.5), kind=kOutput, calls=%fused_computation.13 | convolution fusion | flops 410779648 | bytes 3670016 | tf_op jit(solution)/shard_map/dot_general | solution.py:29
  21.6 1.3 copy.31
  22.8 4.4 %reshape_reshape.3 = bf16[8,128,2,384]{3,2,1,0:T(2,128)(2,1)} reshape(bf16[8,8,16,768]{3,2,1,0:T(8,128)(2,1)} %bitcast.48) | data formatting | bytes 3145728 | tf_op jit(solution)/shard_map/reshape;reshape | solution.py:61
  27.2 2.8 %copy.29 = bf16[8,2,128,384]{3,2,1,0:T(8,128)(2,1)} copy(bf16[8,2,128,384]{3,1,2,0:T(2,128)(2,1)} %bitcast.49) | data formatting | bytes 3145728 | tf_op jit(solution)/shard_map/transpose | solution.py:62
  30.0 0.0 all-to-all-done
  30.0 6.0 %all-to-all-start.2 = ((bf16[16,128,384]{2,1,0:T(8,128)(2,1)}), bf16[16,128,384]{2,1,0:T(8,128)(2,1)}, u32[]{:S(2)}, u32[]{:S(2)}) async-start(bf16[16,128,384]{2,1,0:T(8,128)(2,1)} %bitcast.47), calls=%async_computation.2 | async-start | bytes 3145728 | tf_op jit(solution)/shard_map/all_to_all | solution.py:65
  36.1 0.0 all-gather.5.cloned.1.call-start
  36.1 0.1 fusion.16
  36.2 0.4 select_reduce_fusion
  36.6 67.7 %all-to-all-done.2 = bf16[16,128,384]{2,1,0:T(8,128)(2,1)} async-done(((bf16[16,128,384]{2,1,0:T(8,128)(2,1)}), bf16[16,128,384]{2,1,0:T(8,128)(2,1)}, u32[]{:S(2)}, u32[]{:S(2)}) %all-to-all-start.2) | async-done | bytes 1572896 | tf_op jit(solution)/shard_map/all_to_all | solution.py:65
  104.4 1.0 all-gather.3.cloned.1.call-done
  105.4 8.5 %convolution_convert_fusion.1 = bf16[384,2048]{1,0:T(8,128)(2,1)} fusion(bf16[2048,384]{1,0:T(8,128)(2,1)} %bitcast.17, bf16[2048,2048]{1,0:T(8,128)(2,1)} %all-gather.3.cloned.1.call-done), kind=kOutput, calls=%fused_computation.11 | convolution fusion | flops 3222011904 | bytes 11534336 | tf_op jit(solution)/shard_map/dot_general | solution.py:96
  113.9 0.0 all-gather.5.cloned.1.call-update
  113.9 4.9 %multiply_convert_fusion = bf16[16,80,2048]{2,1,0:T(8,128)(2,1)S(1)} fusion(f32[16,80]{1,0:T(8,128)S(1)} %select_reduce_fusion, bf16[16,128,2048]{2,1,0:T(8,128)(2,1)} %bitcast.45, s32[16,128]{1,0:T(8,128)S(1)} %fusion.16), kind=kOutput, calls=%fused_computation | convolution fusion | flops 676495360 | bytes 13644800 | tf_op jit(solution)/shard_map/dot_general | solution.py:77
  118.8 0.0 copy-done
  118.8 5.6 %convolution_convert_fusion = bf16[1280,768]{1,0:T(8,128)(2,1)} fusion(bf16[1280,2048]{1,0:T(8,128)(2,1)S(1)} %bitcast.46, bf16[1,768,2048]{2,1,0:T(8,128)(2,1)S(1)} %copy-done), kind=kOutput, calls=%fused_computation.4 | convolution fusion | flops 4027514880 | bytes 10354688 | tf_op jit(solution)/shard_map/dot_general | solution.py:85
  124.4 9.3 %all-to-all-start.1 = ((bf16[16,80,768]{2,1,0:T(8,128)(2,1)}), bf16[16,80,768]{2,1,0:T(8,128)(2,1)}, u32[]{:S(2)}, u32[]{:S(2)}) async-start(bf16[16,80,768]{2,1,0:T(8,128)(2,1)} %bitcast.50), calls=%async_computation.1 | async-start | bytes 3932160 | tf_op jit(solution)/shard_map/all_to_all | solution.py:91
  133.7 0.1 copy.24
  133.8 0.1 eq.82
  133.9 0.0 all-gather.5.cloned.1.call-done
  134.0 0.0 copy-start.1
  134.0 4.8 %fusion.15 = bf16[1,384,768]{2,1,0:T(8,128)(2,1)} fusion(bf16[384,2048]{1,0:T(8,128)(2,1)} %convolution_convert_fusion.1, bf16[768,2048]{1,0:T(8,128)(2,1)} %all-gather.5.cloned.1.call-done), kind=kOutput, calls=%fused_computation.20 | convolution fusion | flops 1208549376 | bytes 5308416 | tf_op jit(solution)/shard_map/dot_general | solution.py:104
  138.7 0.0 copy-done.1
  138.7 5.1 %fusion.1 = bf16[1,1024,2048]{2,1,0:T(8,128)(2,1)} fusion(bf16[768,2048]{1,0:T(8,128)(2,1)S(1)} %copy-done.1, s32[]{:T(128)S(6)} %select_n.49), kind=kOutput, calls=%fused_computation.5 | convolution fusion | flops 3225419776 | bytes 8912900 | tf_op jit(solution)/shard_map/dot_general | solution.py:112
  143.8 34.3 %all-to-all-done.1 = bf16[16,80,768]{2,1,0:T(8,128)(2,1)} async-done(((bf16[16,80,768]{2,1,0:T(8,128)(2,1)}), bf16[16,80,768]{2,1,0:T(8,128)(2,1)}, u32[]{:S(2)}, u32[]{:S(2)}) %all-to-all-start.1) | async-done | bytes 1966112 | tf_op jit(solution)/shard_map/all_to_all | solution.py:91
  178.2 5.1 %fusion.13 = bf16[128,8,768]{2,1,0:T(8,128)(2,1)} fusion(bf16[1280,768]{1,0:T(8,128)(2,1)} %bitcast.8, s32[1024]{0:T(1024)S(1)} %eq.82), kind=kOutput, calls=%fused_computation.17 | convolution fusion | flops 2015363072 | bytes 3543040 | tf_op jit(solution)/shard_map/dot_general | solution.py:128
  (6 shorter events, 0.0 us)
Async XLA Ops:
  7.2 111.7 %copy-start = (bf16[1,768,2048]{2,1,0:T(8,128)(2,1)S(1)}, bf16[1,768,2048]{2,1,0:T(8,128)(2,1)}, u32[]{:S(2)}) copy-start(bf16[1,768,2048]{2,1,0:T(8,128)(2,1)} %param.9) | copy-start | bytes 9437188
  7.2 98.2 %all-gather.3.cloned.1.call-start = ((), (), s32[]{:S(2)}) async-start(), calls=%async_computation.3 | async-start | bytes 8912896 | tf_op jit(solution)/shard_map/all_gather | solution.py:51
  9.4 20.6 %all-to-all-start = ((f32[16,1,128]{2,1,0:T(1,128)}), f32[16,1,128]{2,1,0:T(1,128)S(1)}, u32[]{:S(2)}, u32[]{:S(2)}) async-start(f32[16,1,128]{2,1,0:T(1,128)} %bitcast.2), calls=%async_computation | async-start | bytes 16384 | tf_op jit(solution)/shard_map/all_to_all | solution.py:56
  30.0 74.3 %all-to-all-start.2 = ((bf16[16,128,384]{2,1,0:T(8,128)(2,1)}), bf16[16,128,384]{2,1,0:T(8,128)(2,1)}, u32[]{:S(2)}, u32[]{:S(2)}) async-start(bf16[16,128,384]{2,1,0:T(8,128)(2,1)} %bitcast.47), calls=%async_computation.2 | async-start | bytes 3145728 | tf_op jit(solution)/shard_map/all_to_all | solution.py:65
  36.1 97.9 %all-gather.5.cloned.1.call-start = ((), (), s32[]{:S(2)}) async-start(), calls=%async_computation.4 | async-start | bytes 4718592 | tf_op jit(solution)/shard_map/all_gather | solution.py:102
  124.4 53.7 %all-to-all-start.1 = ((bf16[16,80,768]{2,1,0:T(8,128)(2,1)}), bf16[16,80,768]{2,1,0:T(8,128)(2,1)}, u32[]{:S(2)}, u32[]{:S(2)}) async-start(bf16[16,80,768]{2,1,0:T(8,128)(2,1)} %bitcast.50), calls=%async_computation.1 | async-start | bytes 3932160 | tf_op jit(solution)/shard_map/all_to_all | solution.py:91
  134.0 4.8 %copy-start.1 = (bf16[768,2048]{1,0:T(8,128)(2,1)S(1)}, bf16[768,2048]{1,0:T(8,128)(2,1)}, u32[]{:S(2)}) copy-start(bf16[768,2048]{1,0:T(8,128)(2,1)} %all-gather.5.cloned.1.call-done) | copy-start | bytes 9437188
Sparse Core Ops, SparseCore 0:
  10.2 95.1 all-gather.2
  114.0 15.9 all-gather.4

commit v2 on v1

--- a/solution.py
+++ b/solution.py
@@ -1,6 +1,9 @@
+import functools
 import jax
 import jax.numpy as jnp
 from jax import lax
+from jax.experimental import pallas as pl
+from jax.experimental.pallas import tpu as pltpu
 from jax.sharding import PartitionSpec as P
 
 AXES = ("ep", "dp")
@@ -134,9 +137,362 @@
     return (hidden_grad, left.astype(jnp.bfloat16)[None], right.astype(jnp.bfloat16)[None])
 
 
+def exchange_kernel(
+    ep_count, dp_count, capacity,
+    grad_hbm, hidden_hbm, weight_hbm, gate_out, gate_pairs, host_pairs,
+    ret_hbm, left_hbm, right_hbm,
+    shards, weight, hidden, gate_in, place, sum_out, sum_in, sum_t, rows, ret_out,
+    full, cols_t, left, right,
+    local_sem, out_sem, o_send, o_recv, g_send, g_recv, c_send, c_recv, r_send, r_recv, x_send, x_recv,
+):
+    e = lax.axis_index("ep")
+    c = lax.axis_index("dp")
+    z, x = e // 2, e % 2
+    lines = ep_count // 2
+    count = ep_count * dp_count
+    me = e * dp_count + c
+    tokens, width = shards.shape[1:]
+    hidden_width = weight.shape[0]
+    half = hidden_width // dp_count
+
+    def at(device):
+        return {"ep": device // dp_count, "dp": device % dp_count}
+
+    def index(line, column, core):
+        return (line * 2 + column) * dp_count + core
+
+    def remote(src, dst, send, recv, device):
+        return pltpu.make_async_remote_copy(
+            src_ref=src, dst_ref=dst, send_sem=send, recv_sem=recv,
+            device_id=at(device), device_id_type=pl.DeviceIdType.MESH,
+        )
+
+    def each_peer(body):
+        def step(d, carry):
+            body(lax.rem(me + d, count))
+            return carry
+        lax.fori_loop(1, count, step, 0)
+
+    loads = [
+        pltpu.make_async_copy(grad_hbm, shards.at[me], local_sem.at[0]),
+        pltpu.make_async_copy(hidden_hbm, hidden, local_sem.at[1]),
+        pltpu.make_async_copy(weight_hbm, weight, local_sem.at[2]),
+    ]
+    for load in loads:
+        load.start()
+
+    barrier = pltpu.get_barrier_semaphore()
+    each_peer(lambda peer: pl.semaphore_signal(
+        barrier, inc=1, device_id=at(peer), device_id_type=pl.DeviceIdType.MESH))
+    pl.semaphore_wait(barrier, count - 1)
+
+    def gate_copy(peer):
+        return remote(gate_out.at[peer], gate_in.at[me], g_send.at[peer], g_recv.at[me], peer)
+
+    def sum_copy(peer):
+        return remote(sum_out.at[peer], sum_in.at[me], c_send.at[peer], c_recv.at[me], peer)
+
+    def ret_copy(peer):
+        return remote(ret_out.at[peer], ret_hbm.at[me], r_send.at[peer], r_recv.at[me], peer)
+
+    def shard_copy(route, shard, device):
+        return remote(shards.at[shard], shards.at[shard], o_send.at[route, shard], o_recv.at[shard], device)
+
+    def wait_shard(shard):
+        shard_copy(0, shard, (me + 1) % count).wait_recv()
+
+    def relay(line, action):
+        shard = index(line, x, c)
+
+        @pl.when((line <= z) & (z + 1 < lines))
+        def _():
+            action(shard_copy(0, shard, index(z + 1, x, c)))
+
+        @pl.when((line >= z) & (z >= 1))
+        def _():
+            action(shard_copy(1, shard, index(z - 1, x, c)))
+
+        action(shard_copy(2, shard, index(z, 1 - x, c)))
+        action(shard_copy(3, shard, index(z, x, 1 - c)))
+
+    def cross(line, action):
+        action(shard_copy(3, index(line, 1 - x, c), index(z, x, 1 - c)))
+
+    start = lambda copy: copy.start()
+    each_peer(lambda peer: gate_copy(peer).start())
+    loads[0].wait()
+    relay(z, start)
+    gate_in[me] = gate_out[me]
+
+    loads[1].wait()
+    block = gate_pairs.shape[2]
+    per = tokens // gate_pairs.shape[0]
+    choose = block // per
+    line_of = lax.broadcasted_iota(jnp.int32, (ep_count * per, block), 0)
+    lane_of = lax.broadcasted_iota(jnp.int32, (ep_count * per, block), 1)
+    own = (lane_of // choose) == (line_of % per)
+
+    def sum_block(b, carry):
+        keep = own & (host_pairs[b] == line_of // per)
+        exact = jnp.where(keep, gate_pairs[b], 0.0)
+        high = exact.astype(jnp.bfloat16)
+        low = (exact - high.astype(jnp.float32)).astype(jnp.bfloat16)
+        values = hidden[pl.ds(pl.multiple_of(b * block, block), block), :]
+        out = jnp.dot(high, values, preferred_element_type=jnp.float32)
+        out = (out + jnp.dot(low, values, preferred_element_type=jnp.float32)).astype(jnp.bfloat16)
+        for host in range(ep_count):
+            for core in range(dp_count):
+                sum_out[host * dp_count + core, pl.ds(pl.multiple_of(b * per, per), per), :] = out[
+                    host * per:(host + 1) * per, core * half:(core + 1) * half]
+        return carry
+
+    lax.fori_loop(0, gate_pairs.shape[0], sum_block, 0)
+    own_sum = pltpu.make_async_copy(sum_out.at[me], sum_in.at[me], local_sem.at[1])
+    own_sum.start()
+    each_peer(lambda peer: sum_copy(peer).start())
+
+    each_peer(lambda peer: gate_copy(peer).wait_send())
+    each_peer(lambda peer: remote(
+        gate_out.at[peer], gate_in.at[peer], g_send.at[peer], g_recv.at[peer], peer).wait_recv())
+    gates = gate_in[:, 0, :]
+    used = gates > 0
+    before = (
+        lax.broadcasted_iota(jnp.int32, (tokens, tokens), 0)
+        < lax.broadcasted_iota(jnp.int32, (tokens, tokens), 1)
+    ).astype(jnp.float32).astype(jnp.bfloat16)
+    earlier = jnp.dot(
+        used.astype(jnp.float32).astype(jnp.bfloat16), before, preferred_element_type=jnp.float32)
+    place[:, 0, :] = jnp.where(used, earlier, -1.0)
+    loads[2].wait()
+
+    rank = lax.broadcasted_iota(jnp.int32, (capacity, tokens), 0).astype(jnp.float32)
+    tile = 256
+
+    def serve(line):
+        first = index(line, 0, 0)
+        number = 2 * dp_count
+
+        def gather(i, carry):
+            shard = first + i
+            select = place[shard] == rank
+            picked = jnp.dot(
+                jnp.where(select, 1.0, 0.0).astype(jnp.bfloat16), shards[shard],
+                preferred_element_type=jnp.float32)
+            gate = jnp.sum(jnp.where(select, gate_in[shard], 0.0), axis=1, keepdims=True)
+            rows[i] = (picked * gate).astype(jnp.bfloat16)
+            return carry
+
+        lax.fori_loop(0, number, gather, 0)
+
+        def product(n, carry):
+            lanes = pl.ds(pl.multiple_of(n * tile, tile), tile)
+            out = lax.dot_general(
+                rows[...].reshape(number * capacity, width), weight[lanes, :],
+                (((1,), (1,)), ((), ())), preferred_element_type=jnp.float32)
+            ret_out[pl.ds(first, number), :, lanes] = out.astype(jnp.bfloat16).reshape(
+                number, capacity, tile)
+            return carry
+
+        lax.fori_loop(0, hidden_width // tile, product, 0)
+
+        def send(i, carry):
+            shard = first + i
+
+            @pl.when(shard != me)
+            def _():
+                ret_copy(shard).start()
+
+            @pl.when(shard == me)
+            def _():
+                pltpu.make_async_copy(ret_out.at[me], ret_hbm.at[me], local_sem.at[0]).start()
+
+            return carry
+
+        lax.fori_loop(0, number, send, 0)
+
+    def inside(line, body):
+        @pl.when((line >= 0) & (line < lines))
+        def _():
+            body(line)
+
+    def take_line(line):
+        wait_shard(index(line, x, c))
+        relay(line, start)
+
+    def take_cross(line):
+        wait_shard(index(line, 1 - x, c))
+        cross(line, start)
+
+    side = 1 - 2 * (z // 2)
+    second = z + side
+    fourth = 3 * (1 - z // 2)
+    order = [z, second, 6 - z - second - fourth, fourth]
+    for level in range(1, lines + 1):
+        if level < lines:
+            inside(z - level, take_line)
+            inside(z + level, take_line)
+        if level == 1:
+            take_cross(z)
+        else:
+            inside(z - level + 1, take_cross)
+            inside(z + level - 1, take_cross)
+        line = order[level - 1]
+        wait_shard(index(line, 0, 1 - c))
+        wait_shard(index(line, 1, 1 - c))
+        serve(line)
+
+    own_sum.wait()
+    each_peer(lambda peer: remote(
+        sum_out.at[peer], sum_in.at[peer], c_send.at[peer], c_recv.at[peer], peer).wait_recv())
+
+    def turn(j, carry):
+        sum_t[:, pl.ds(pl.multiple_of(j * tokens, tokens), tokens)] = sum_in[j].T
+        return carry
+
+    lax.fori_loop(0, count, turn, 0)
+    mine = pl.ds(pl.multiple_of(c * half, half), half)
+
+    def grad_tile(n, carry):
+        lanes = pl.ds(pl.multiple_of(n * tile, tile), tile)
+        full[mine, lanes] = jnp.dot(
+            sum_t[...], shards[:, :, lanes].reshape(count * tokens, tile),
+            preferred_element_type=jnp.float32).astype(jnp.bfloat16)
+        return carry
+
+    lax.fori_loop(0, width // tile, grad_tile, 0)
+    swap = remote(full.at[mine], full.at[mine], x_send, x_recv, index(z, x, 1 - c))
+    swap.start()
+    swap.wait()
+
+    part = width // dp_count
+    cols_t[...] = full[:, pl.ds(pl.multiple_of(c * part, part), part)].T
+    left[...] = (
+        lax.dot_general(
+            full[mine, :], full[...], (((1,), (1,)), ((), ())), preferred_element_type=jnp.float32)
+        / width
+    ).astype(jnp.bfloat16)
+    left_copy = pltpu.make_async_copy(left, left_hbm, out_sem.at[0])
+    left_copy.start()
+
+    def right_tile(n, carry):
+        lanes = pl.ds(pl.multiple_of(n * tile, tile), tile)
+        right[:, lanes] = (
+            jnp.dot(cols_t[...], full[:, lanes], preferred_element_type=jnp.float32) / hidden_width
+        ).astype(jnp.bfloat16)
+        return carry
+
+    lax.fori_loop(0, width // tile, right_tile, 0)
+    right_copy = pltpu.make_async_copy(right, right_hbm, out_sem.at[1])
+    right_copy.start()
+
+    each_peer(lambda peer: remote(
+        ret_out.at[peer], ret_hbm.at[peer], r_send.at[peer], r_recv.at[peer], peer).wait_recv())
+    pltpu.make_async_copy(ret_out.at[me], ret_hbm.at[me], local_sem.at[0]).wait()
+    each_peer(lambda peer: sum_copy(peer).wait_send())
+    each_peer(lambda peer: ret_copy(peer).wait_send())
+    wait_send = lambda copy: copy.wait_send()
+    for line in range(lines):
+        relay(line, wait_send)
+        cross(line, wait_send)
+    left_copy.wait()
+    right_copy.wait()
+
+
+def exchange(out_grad, saved_hidden, weight, dense_gate, gate_pairs, host_pairs, ep_count, dp_count, capacity):
+    tokens, width = out_grad.shape
+    pairs, hidden_width = saved_hidden.shape
+    count = ep_count * dp_count
+    half, part = hidden_width // dp_count, width // dp_count
+    bf16, f32 = jnp.bfloat16, jnp.float32
+    dma = pltpu.SemaphoreType.DMA
+    anywhere = pl.BlockSpec(memory_space=pl.ANY)
+    vmem = pl.BlockSpec(memory_space=pltpu.VMEM)
+    return pl.pallas_call(
+        functools.partial(exchange_kernel, ep_count, dp_count, capacity),
+        out_shape=(
+            jax.ShapeDtypeStruct((count, capacity, hidden_width), bf16),
+            jax.ShapeDtypeStruct((half, hidden_width), bf16),
+            jax.ShapeDtypeStruct((part, width), bf16),
+        ),
+        in_specs=[anywhere] * 3 + [vmem] * 3,
+        out_specs=(anywhere,) * 3,
+        scratch_shapes=[
+            pltpu.VMEM((count, tokens, width), bf16),
+            pltpu.VMEM((hidden_width, width), bf16),
+            pltpu.VMEM((pairs, hidden_width), bf16),
+            pltpu.VMEM((count, 1, tokens), f32),
+            pltpu.VMEM((count, 1, tokens), f32),
+            pltpu.VMEM((count, tokens, half), bf16),
+            pltpu.VMEM((count, tokens, half), bf16),
+            pltpu.VMEM((half, count * tokens), bf16),
+            pltpu.VMEM((2 * dp_count, capacity, width), bf16),
+            pltpu.VMEM((count, capacity, hidden_width), bf16),
+            pltpu.VMEM((hidden_width, width), bf16),
+            pltpu.VMEM((part, hidden_width), bf16),
+            pltpu.VMEM((half, hidden_width), bf16),
+            pltpu.VMEM((part, width), bf16),
+            dma((3,)), dma((2,)), dma((4, count)), dma((count,)), dma((count,)), dma((count,)),
+            dma((count,)), dma((count,)), dma((count,)), dma((count,)), dma, dma,
+        ],
+        compiler_params=pltpu.CompilerParams(
+            collective_id=0, has_side_effects=True, vmem_limit_bytes=56 << 20),
+        cost_estimate=pl.CostEstimate(
+            flops=16_000_000_000, bytes_accessed=20_000_000, transcendentals=0),
+    )(out_grad, saved_hidden, weight, dense_gate, gate_pairs, host_pairs)
+
+
+def restore(returned, named, before, capacity):
+    tokens, choose, slot_count = named.shape
+    hidden_width = returned.shape[2]
+    slots = jnp.arange(slot_count, dtype=jnp.int32)
+    served = jnp.any(named, axis=1).astype(jnp.bfloat16)
+    earlier = lax.dot_general(
+        before, served, (((0,), (0,)), ((), ())), preferred_element_type=jnp.float32
+    ).astype(jnp.int32)
+    position = jnp.sum(
+        jnp.where(named, (earlier + slots * capacity)[:, None, :], 0), axis=2
+    ).reshape(tokens * choose)
+    pick = (
+        position[:, None] == jnp.arange(slot_count * capacity, dtype=jnp.int32)[None, :]
+    ).astype(jnp.bfloat16)
+    return lax.dot_general(
+        pick,
+        returned.reshape(slot_count * capacity, hidden_width),
+        (((1,), (0,)), ((), ())),
+        preferred_element_type=jnp.float32,
+    ).astype(jnp.bfloat16).reshape(tokens, choose, hidden_width)
+
+
+def fused(out_grad, gate_prob, saved_hidden, slot_weight, pair_slot, slot_expert):
+    tokens, choose = pair_slot.shape
+    slot_count = slot_expert.shape[0]
+    ep_count = lax.axis_size("ep")
+    dp_count = lax.axis_size("dp")
+    capacity = max(2, 5 * tokens * choose // (4 * slot_count))
+    slots = jnp.arange(slot_count, dtype=jnp.int32)
+    named = pair_slot[:, :, None] == slots[None, None, :]
+    dense_gate = jnp.sum(jnp.where(named, gate_prob[:, :, None], 0.0), axis=1).T
+    expert_of_pair = jnp.sum(jnp.where(named, slot_expert[None, None, :], 0), axis=2)
+    blocks = tokens // BLOCK
+    returned, left, right = exchange(
+        out_grad,
+        saved_hidden.reshape(tokens * choose, saved_hidden.shape[2]),
+        slot_weight[0],
+        dense_gate[:, None, :],
+        gate_prob.reshape(blocks, 1, BLOCK * choose),
+        expert_of_pair.reshape(blocks, 1, BLOCK * choose),
+        ep_count, dp_count, capacity,
+    )
+    before = (
+        jnp.arange(tokens)[:, None] < jnp.arange(tokens)[None, :]
+    ).astype(jnp.bfloat16)
+    return restore(returned, named, before, capacity), left[None], right[None]
+
+
 def solution(mesh):
+    fits = mesh.shape["ep"] == 8 and mesh.shape["dp"] == 2
     return jax.shard_map(
-        local,
+        fused if fits else local,
         mesh=mesh,
         in_specs=(
             P(("groups", "ep", "dp"), None),

time: 191 us -> 142 us (0.74)
  the two profiles are of different devices: /device:TPU:21 before, /device:TPU:3 now
where the time goes in v2:
time: 142 us; the launch traced here: 141 us
  Pallas kernels  127 us (89%)
  matrix products  5.34 us (4%)
  local copies, waits for them, and re-layouts  5.28 us (4%)
  other arithmetic  2.84 us (2%)
    pallas_call x1, Pallas kernels, exchange(): pl.pallas_call(functools.partial(exchange_kernel, ep_count, dp_count, cap...  127 us
    dot_general x1, matrix products, restore(): lax.dot_general(pick, returned.reshape(slot_count * capacity, hidden_widt...  5.24 us
    unnamed x7, local copies, waits for them, and re-layouts  3.62 us

profile of v2, /device:TPU:3, one launch (start us, length us, event | category | flops | bytes accessed | tf_op | source)
XLA Modules:
  0.0 141.4 jit_solution(10690185620556747069)
XLA Ops:
  0.6 0.7 fusion.5
  1.3 0.1 fusion.4
  1.4 0.8 select_reduce_fusion.2
  2.3 1.3 select_reduce_fusion.1
  3.6 0.1 copy.19
  3.7 0.1 eq.31
  3.8 0.1 copy.21
  3.9 0.7 reshape.32
  4.6 0.8 copy.20
  5.3 0.7 reshape.31
  6.0 127.3 %shard_map.85 = (bf16[16,80,768]{2,1,0:T(8,128)(2,1)}, bf16[384,768]{1,0:T(8,128)(2,1)}, bf16[1024,2048]{1,0:T(8,128)(2,1)}) custom-call(bf16[128,2048]{1,0:T(8,128)(2,1)} %grad_hbm.1, bf16[1024,768]{1,0:T(8,128)(2,1)} %bitcast.20, bf16[768,2048]{1,0:T(8,128)(2,1)} %bitcast.19, f32[16,1,128]{2,1,0:T(1,128)} %bitcast.16, f32[8,1,128]{2,1,0:T(1,128)} %bitcast.18, ...), custom_call_target="tpu_custom_call" | custom-call | flops 16000000000 | bytes 20000000 | tf_op jit(solution)/shard_map/pallas_call | solution.py:410
  133.3 0.0 copy-start.1
  133.3 0.0 copy-start
  133.3 5.2 %fusion.3 = bf16[128,8,768]{2,1,0:T(8,128)(2,1)} fusion(bf16[1280,768]{1,0:T(8,128)(2,1)} %bitcast.21, s32[1024]{0:T(1024)S(1)} %eq.31), kind=kOutput, calls=%fused_computation.4 | convolution fusion | flops 2015363072 | bytes 3543040 | tf_op jit(solution)/shard_map/dot_general | solution.py:458
  138.6 0.0 copy-done.1
  138.6 0.8 copy.26
  139.4 0.0 copy-done
  139.4 2.0 %copy.27 = bf16[1,1024,2048]{2,1,0:T(8,128)(2,1)} copy(bf16[1,1024,2048]{2,1,0:T(8,128)(2,1)S(1)} %bitcast.14) | data formatting | bytes 8388608
  (1 shorter events, 0.0 us)
Async XLA Ops:
  133.3 5.3 %copy-start.1 = (bf16[384,768]{1,0:T(8,128)(2,1)S(1)}, bf16[384,768]{1,0:T(8,128)(2,1)}, u32[]{:S(2)}) copy-start(bf16[384,768]{1,0:T(8,128)(2,1)} %get-tuple-element.7) | copy-start | bytes 1769476
  133.3 6.1 %copy-start = (bf16[1024,2048]{1,0:T(8,128)(2,1)S(1)}, bf16[1024,2048]{1,0:T(8,128)(2,1)}, u32[]{:S(2)}) copy-start(bf16[1024,2048]{1,0:T(8,128)(2,1)} %get-tuple-element.8) | copy-start | bytes 12582916

commit v3 on v2

--- a/solution.py
+++ b/solution.py
@@ -8,6 +8,13 @@
 
 AXES = ("ep", "dp")
 BLOCK = 16
+CHUNKS = 2
+PLAN = (
+    ("line cross", 1), ("across", 0), ("serve", 0),
+    ("line cross", 2), ("serve", 1), ("near", 0),
+    ("line cross", 3), ("serve", 2),
+    ("cross", 4), ("serve", 3),
+)
 
 
 def combined(gate_prob, expert_of_pair, saved_hidden, experts):
@@ -173,6 +180,18 @@
             return carry
         lax.fori_loop(1, count, step, 0)
 
+    def each_across(body):
+        def step(d, carry):
+            body((1 - me // (count // 2)) * (count // 2) + lax.rem(me + d, count // 2))
+            return carry
+        lax.fori_loop(0, count // 2, step, 0)
+
+    def each_near(body):
+        def step(d, carry):
+            body(me // (count // 2) * (count // 2) + lax.rem(me + d, count // 2))
+            return carry
+        lax.fori_loop(1, count // 2, step, 0)
+
     loads = [
         pltpu.make_async_copy(grad_hbm, shards.at[me], local_sem.at[0]),
         pltpu.make_async_copy(hidden_hbm, hidden, local_sem.at[1]),
@@ -195,33 +214,38 @@
     def ret_copy(peer):
         return remote(ret_out.at[peer], ret_hbm.at[me], r_send.at[peer], r_recv.at[me], peer)
 
-    def shard_copy(route, shard, device):
-        return remote(shards.at[shard], shards.at[shard], o_send.at[route, shard], o_recv.at[shard], device)
-
-    def wait_shard(shard):
-        shard_copy(0, shard, (me + 1) % count).wait_recv()
-
-    def relay(line, action):
+    piece = tokens // CHUNKS
+
+    def shard_copy(route, shard, chunk, device):
+        held = shards.at[shard, pl.ds(chunk * piece, piece)]
+        return remote(
+            held, held, o_send.at[route, chunk, shard], o_recv.at[chunk, shard], device)
+
+    def wait_shard(shard, chunk):
+        shard_copy(0, shard, chunk, (me + 1) % count).wait_recv()
+
+    def relay(line, chunk, action):
         shard = index(line, x, c)
 
         @pl.when((line <= z) & (z + 1 < lines))
         def _():
-            action(shard_copy(0, shard, index(z + 1, x, c)))
+            action(shard_copy(0, shard, chunk, index(z + 1, x, c)))
 
         @pl.when((line >= z) & (z >= 1))
         def _():
-            action(shard_copy(1, shard, index(z - 1, x, c)))
-
-        action(shard_copy(2, shard, index(z, 1 - x, c)))
-        action(shard_copy(3, shard, index(z, x, 1 - c)))
-
-    def cross(line, action):
-        action(shard_copy(3, index(line, 1 - x, c), index(z, x, 1 - c)))
+            action(shard_copy(1, shard, chunk, index(z - 1, x, c)))
+
+        action(shard_copy(2, shard, chunk, index(z, 1 - x, c)))
+        action(shard_copy(3, shard, chunk, index(z, x, 1 - c)))
+
+    def cross(line, chunk, action):
+        action(shard_copy(3, index(line, 1 - x, c), chunk, index(z, x, 1 - c)))
 
     start = lambda copy: copy.start()
     each_peer(lambda peer: gate_copy(peer).start())
     loads[0].wait()
-    relay(z, start)
+    for chunk in range(CHUNKS):
+        relay(z, chunk, start)
     gate_in[me] = gate_out[me]
 
     loads[1].wait()
@@ -249,7 +273,6 @@
     lax.fori_loop(0, gate_pairs.shape[0], sum_block, 0)
     own_sum = pltpu.make_async_copy(sum_out.at[me], sum_in.at[me], local_sem.at[1])
     own_sum.start()
-    each_peer(lambda peer: sum_copy(peer).start())
 
     each_peer(lambda peer: gate_copy(peer).wait_send())
     each_peer(lambda peer: remote(
@@ -310,36 +333,47 @@
 
         lax.fori_loop(0, number, send, 0)
 
-    def inside(line, body):
+    def inside(line, chunk, body):
         @pl.when((line >= 0) & (line < lines))
         def _():
-            body(line)
-
-    def take_line(line):
-        wait_shard(index(line, x, c))
-        relay(line, start)
-
-    def take_cross(line):
-        wait_shard(index(line, 1 - x, c))
-        cross(line, start)
+            body(line, chunk)
+
+    def take_line(line, chunk):
+        wait_shard(index(line, x, c), chunk)
+        relay(line, chunk, start)
+
+    def take_cross(line, chunk):
+        wait_shard(index(line, 1 - x, c), chunk)
+        cross(line, chunk, start)
 
     side = 1 - 2 * (z // 2)
     second = z + side
     fourth = 3 * (1 - z // 2)
     order = [z, second, 6 - z - second - fourth, fourth]
-    for level in range(1, lines + 1):
-        if level < lines:
-            inside(z - level, take_line)
-            inside(z + level, take_line)
-        if level == 1:
-            take_cross(z)
+    def both(line_below, line_above, chunk, body):
+        inside(line_below, chunk, body)
+        inside(line_above, chunk, body)
+
+    for event, level in PLAN:
+        if event == "across":
+            each_across(lambda peer: sum_copy(peer).start())
+        elif event == "near":
+            each_near(lambda peer: sum_copy(peer).start())
+        elif event == "serve":
+            line = order[level]
+            for chunk in range(CHUNKS):
+                wait_shard(index(line, 0, 1 - c), chunk)
+                wait_shard(index(line, 1, 1 - c), chunk)
+            serve(line)
         else:
-            inside(z - level + 1, take_cross)
-            inside(z + level - 1, take_cross)
-        line = order[level - 1]
-        wait_shard(index(line, 0, 1 - c))
-        wait_shard(index(line, 1, 1 - c))
-        serve(line)
+            for chunk in range(CHUNKS):
+                if "line" in event:
+                    both(z - level, z + level, chunk, take_line)
+                if "cross" in event:
+                    if level == 1:
+                        take_cross(z, chunk)
+                    else:
+                        both(z - level + 1, z + level - 1, chunk, take_cross)
 
     own_sum.wait()
     each_peer(lambda peer: remote(
@@ -391,9 +425,10 @@
     each_peer(lambda peer: sum_copy(peer).wait_send())
     each_peer(lambda peer: ret_copy(peer).wait_send())
     wait_send = lambda copy: copy.wait_send()
-    for line in range(lines):
-        relay(line, wait_send)
-        cross(line, wait_send)
+    for chunk in range(CHUNKS):
+        for line in range(lines):
+            relay(line, chunk, wait_send)
+            cross(line, chunk, wait_send)
     left_copy.wait()
     right_copy.wait()
 
@@ -431,7 +466,7 @@
             pltpu.VMEM((part, hidden_width), bf16),
             pltpu.VMEM((half, hidden_width), bf16),
             pltpu.VMEM((part, width), bf16),
-            dma((3,)), dma((2,)), dma((4, count)), dma((count,)), dma((count,)), dma((count,)),
+            dma((3,)), dma((2,)), dma((4, CHUNKS, count)), dma((CHUNKS, count)), dma((count,)), dma((count,)),
             dma((count,)), dma((count,)), dma((count,)), dma((count,)), dma, dma,
         ],
         compiler_params=pltpu.CompilerParams(

time: 142 us -> 128 us (0.901)
  the two profiles are of different devices: /device:TPU:3 before, /device:TPU:21 now
where the time goes in v3:
time: 128 us; the launch traced here: 127 us
  Pallas kernels  112 us (88%)
  matrix products  5.34 us (4%)
  local copies, waits for them, and re-layouts  5.28 us (4%)
  other arithmetic  2.84 us (2%)
    pallas_call x1, Pallas kernels, exchange(): pl.pallas_call(functools.partial(exchange_kernel, ep_count, dp_count, cap...  112 us
    dot_general x1, matrix products, restore(): lax.dot_general(pick, returned.reshape(slot_count * capacity, hidden_widt...  5.25 us
    unnamed x7, local copies, waits for them, and re-layouts  3.62 us

profile of v3, /device:TPU:21, one launch (start us, length us, event | category | flops | bytes accessed | tf_op | source)
XLA Modules:
  0.0 126.6 jit_solution(2698923416859892498)
XLA Ops:
  0.6 0.7 fusion.5
  1.3 0.1 fusion.4
  1.4 0.8 select_reduce_fusion.2
  2.3 1.3 %select_reduce_fusion.1 = f32[128,16]{0,1:T(8,128)} fusion(f32[128,8]{0,1:T(8,128)} %param.7, s32[128,8]{0,1:T(8,128)} %param.10), kind=kLoop, calls=%fused_computation.8 | loop fusion | flops 47104 | bytes 16384 | tf_op jit(solution)/shard_map/reduce_sum | solution.py:509
  3.6 0.1 copy.19
  3.7 0.1 eq.31
  3.8 0.1 copy.21
  3.9 0.7 reshape.32
  4.6 0.8 copy.20
  5.3 0.7 reshape.31
  6.0 112.4 %shard_map.85 = (bf16[16,80,768]{2,1,0:T(8,128)(2,1)}, bf16[384,768]{1,0:T(8,128)(2,1)}, bf16[1024,2048]{1,0:T(8,128)(2,1)}) custom-call(bf16[128,2048]{1,0:T(8,128)(2,1)} %grad_hbm.1, bf16[1024,768]{1,0:T(8,128)(2,1)} %bitcast.20, bf16[768,2048]{1,0:T(8,128)(2,1)} %bitcast.19, f32[16,1,128]{2,1,0:T(1,128)} %bitcast.16, f32[8,1,128]{2,1,0:T(1,128)} %bitcast.18, ...), custom_call_target="tpu_custom_call" | custom-call | flops 16000000000 | bytes 20000000 | tf_op jit(solution)/shard_map/pallas_call | solution.py:445
  118.5 0.0 copy-start.1
  118.5 0.0 copy-start
  118.5 5.2 %fusion.3 = bf16[128,8,768]{2,1,0:T(8,128)(2,1)} fusion(bf16[1280,768]{1,0:T(8,128)(2,1)} %bitcast.21, s32[1024]{0:T(1024)S(1)} %eq.31), kind=kOutput, calls=%fused_computation.4 | convolution fusion | flops 2015363072 | bytes 3543040 | tf_op jit(solution)/shard_map/dot_general | solution.py:493
  123.7 0.0 copy-done.1
  123.7 0.8 copy.26
  124.5 0.0 copy-done
  124.5 2.0 %copy.27 = bf16[1,1024,2048]{2,1,0:T(8,128)(2,1)} copy(bf16[1,1024,2048]{2,1,0:T(8,128)(2,1)S(1)} %bitcast.14) | data formatting | bytes 8388608
  (1 shorter events, 0.0 us)
Async XLA Ops:
  118.5 5.3 %copy-start.1 = (bf16[384,768]{1,0:T(8,128)(2,1)S(1)}, bf16[384,768]{1,0:T(8,128)(2,1)}, u32[]{:S(2)}) copy-start(bf16[384,768]{1,0:T(8,128)(2,1)} %get-tuple-element.7) | copy-start | bytes 1769476
  118.5 6.1 %copy-start = (bf16[1024,2048]{1,0:T(8,128)(2,1)S(1)}, bf16[1024,2048]{1,0:T(8,128)(2,1)}, u32[]{:S(2)}) copy-start(bf16[1024,2048]{1,0:T(8,128)(2,1)} %get-tuple-element.8) | copy-start | bytes 12582916
